TPU v7x, 32 devices: a whole 2x2x4 slice. The times are simulated.
32 devices in a mesh: row: 8 (over z, x), col: 4 (over y, core).
Axes of the slice: x: 2, y: 2, z: 4, core: 2. Of those that a mesh axis runs over, the one named last changes fastest.
Arguments:
- x_rhs: bfloat16 [16, 1024, 1024], P('col', 'row'), may hold values from -6 to 6
- panel_u: bfloat16 [16, 1024, 256], P('row', 'col'), may hold values from -0.1875 to 0.1875
- panel_v: bfloat16 [16, 1024, 256], P('row', 'col'), may hold values from -0.1875 to 0.1875
- panel_rank: int32 [16], replicated, may hold values from 32 to 256, as said below
- tile_p: bfloat16 [16, 16, 1024, 256], P('row', 'col'), may hold values from -0.09375 to 0.09375
- tile_q: bfloat16 [16, 16, 1024, 256], P('row', 'col'), may hold values from -0.1875 to 0.1875
- tile_rank: int32 [16, 16], P('row', 'col'), may hold values from 32 to 256, as said below
Outputs:
- kriged: bfloat16 [16, 1024, 1024], P('row', None, 'col')
Inputs may be any that keep to these rules, and one draw needn't show every extreme that they name: `panel_rank`: each panel tile's rank; the columns at or beyond it carry no part of the tile. `tile_rank`: each trailing tile's rank; the columns at or beyond it carry no part of the tile.
All inputs are finite; a program needn't handle non-finite values.
Results may differ from a plain program's by a relative error of at most 0.018.
Values may be sent and summed in bfloat16 or wider, within the bound.
A program may use at most 64 MiB of HBM per device.

v0:
```python
import jax
import jax.numpy as jnp
from jax import lax
from jax.sharding import PartitionSpec as P


def shards(x_rhs, panel_u, panel_v, panel_rank, tile_p, tile_q, tile_rank):
    exact = lax.Precision.HIGHEST
    row_at = lax.axis_index("row")
    col_at = lax.axis_index("col")
    t_rows = tile_p.shape[0]
    t_cols = tile_p.shape[1]
    rank_cap = tile_p.shape[3]
    gathered = lax.all_gather(x_rhs, "row", axis=1, tiled=True)
    full_u, full_v = (
        lax.all_gather(panel_u, "col", axis=1, tiled=True),
        lax.all_gather(panel_v, "col", axis=1, tiled=True),
    )
    tile_slot = lax.broadcasted_iota(jnp.int32, (1, 1, rank_cap, 1), 2)
    tile_proj = jnp.einsum("ijbr,jbn->ijrn", tile_q, gathered, preferred_element_type=jnp.float32)
    tile_proj = jnp.where(tile_slot < tile_rank[:, :, None, None], tile_proj, 0.0).astype(
        jnp.bfloat16
    )
    base_sum = jnp.einsum("ijbr,ijrn->ibn", tile_p, tile_proj, preferred_element_type=jnp.float32)
    rank_slot = lax.broadcasted_iota(jnp.int32, (1, rank_cap, 1), 1)
    row_rank = lax.dynamic_slice_in_dim(panel_rank, row_at * t_rows, t_rows)
    row_keep = rank_slot < row_rank[:, None, None]
    u_wide = full_u.astype(jnp.float32)
    tile_ids = row_at * t_rows + jnp.arange(t_rows, dtype=jnp.int32)
    inside = tile_ids // t_cols == col_at
    where_rhs = jnp.clip(tile_ids - col_at * t_cols, 0, t_cols - 1)
    picked = jnp.take(gathered, where_rhs, axis=0)
    keep = jnp.logical_and(inside[:, None, None], row_keep)
    panel_proj = jnp.einsum("jbr,jbn->jrn", full_u, picked, preferred_element_type=jnp.float32)
    panel_proj = jnp.where(keep, panel_proj, 0.0).astype(jnp.bfloat16)
    sweep_part = jnp.einsum("jbr,jrn->bn", full_v, panel_proj, preferred_element_type=jnp.float32)
    sweep_share = lax.psum_scatter(
        sweep_part.astype(jnp.bfloat16), "col", scatter_dimension=1, tiled=True
    )
    sweep = lax.psum(sweep_share, "row").astype(jnp.float32)
    back_proj = jnp.einsum("ibr,bn->irn", full_v.astype(jnp.float32), sweep, precision=exact)
    back_proj = jnp.where(row_keep, back_proj, 0.0)
    late_term = jnp.einsum("ibr,irn->ibn", u_wide, back_proj, precision=exact)
    summed = lax.psum_scatter(
        base_sum.astype(jnp.bfloat16), "col", scatter_dimension=2, tiled=True
    ).astype(jnp.float32)
    return (summed - late_term).astype(jnp.bfloat16)


def solution(mesh):
    return jax.shard_map(
        shards,
        mesh=mesh,
        in_specs=(
            P("col", "row", None),
            P("row", "col", None),
            P("row", "col", None),
            P(),
            P("row", "col", None, None),
            P("row", "col", None, None),
            P("row", "col"),
        ),
        out_specs=P("row", None, "col"),
        check_vma=False,
    )
```

profile of v0, /device:TPU:29, one launch (start us, length us, event | category | flops | bytes accessed | tf_op | source)
XLA Modules:
  0.0 339.8 jit_solution(12860024672213277228)
XLA Ops:
  6.5 0.7 all-gather.4.cloned.1.call-update
  7.3 0.7 all-gather.6.cloned.1.call-update
  8.0 0.0 all-gather.8.cloned.1.call-start
  8.1 0.7 all-gather.8.cloned.1.call-update
  8.7 0.0 reduce-scatter.5.cloned.1.call-start
  8.8 0.7 dynamic_slice.3
  9.6 0.1 iota_compare_fusion.1
  9.7 124.0 %all-gather.4.cloned.1.call-done = bf16[4,1024,1024]{2,1,0:T(8,128)(2,1)} async-done(((bf16[4,128,1024]{2,1,0:T(8,128)(2,1)}), bf16[4,1024,1024]{2,1,0:T(8,128)(2,1)}) %all-gather.4.cloned.1.call-update) | async-done | bytes 8388624 | tf_op jit(solution)/shard_map/all_gather | solution.py:14
  133.7 5.9 %fusion.36 = (bf16[4,512,1024]{2,1,0:T(8,128)(2,1)}, bf16[4,512,1024]{2,1,0:T(8,128)(2,1)}) fusion(bf16[4,1024,1024]{2,1,0:T(8,128)(2,1)} %all-gather.4.cloned.1.call-done), kind=kLoop, calls=%fused_computation.46 | loop fusion | bytes 16777216 | tf_op jit(solution)/shard_map/jit(_take)/gather | solution.py:32
  139.6 2.9 gather_fusion
  142.5 4.4 %gather_fusion.1 = bf16[2,512,1024]{2,1,0:T(8,128)(2,1)} fusion(bf16[4,512,1024]{2,1,0:T(8,128)(2,1)} %get-tuple-element.6, s32[1024]{0:T(1024)S(1)} %pad_clamp_fusion), kind=kCustom, calls=%fused_computation.1 | custom fusion | bytes 4194312 | tf_op jit(solution)/shard_map/jit(_take)/gather | solution.py:32
  146.9 4.5 %all-gather.6.cloned.1.call-done = bf16[2,1024,256]{2,1,0:T(8,128)(2,1)} async-done(((bf16[2,256,256]{2,1,0:T(8,128)(2,1)}), bf16[2,1024,256]{2,1,0:T(8,128)(2,1)}) %all-gather.6.cloned.1.call-update) | async-done | bytes 1048592 | tf_op jit(solution)/shard_map/all_gather | solution.py:16
  151.4 18.3 %all-gather.8.cloned.1.call-done = bf16[2,1024,256]{2,1,0:T(8,128)(2,1)} async-done(((bf16[2,256,256]{2,1,0:T(8,128)(2,1)}), bf16[2,1024,256]{2,1,0:T(8,128)(2,1)}) %all-gather.8.cloned.1.call-update) | async-done | bytes 1048592 | tf_op jit(solution)/shard_map/all_gather | solution.py:17
  169.7 6.1 %fusion.22 = bf16[1024,1024]{0,1:T(8,128)(2,1)} fusion(bf16[2,1024,256]{2,1,0:T(8,128)(2,1)} %all-gather.8.cloned.1.call-done, bf16[2,1024,256]{2,1,0:T(8,128)(2,1)} %all-gather.6.cloned.1.call-done, bf16[2,512,1024]{2,1,0:T(8,128)(2,1)} %gather_fusion.1, bf16[2,512,1024]{2,1,0:T(8,128)(2,1)S(1)} %gather_fusion, pred[2]{0:T(512)(128)(4,1)S(1)} %compare_and_fusion, ...), kind=kOutput, calls=%fused_computation.21 | convolution fusion | flops 2160066560 | bytes 8389122 | tf_op jit(solution)/shard_map/jbr,jrn->bn/dot_general | solution.py:36
  175.9 0.0 all-reduce.2.cloned.1.call-start
  175.9 0.1 iota_compare_fusion
  176.0 31.0 %reduce-scatter.5.cloned.1.call-done = bf16[1024,256]{0,1:T(8,128)(2,1)} async-done(((bf16[1024,1024]{0,1:T(8,128)(2,1)}), bf16[1024,256]{0,1:T(8,128)(2,1)}) %reduce-scatter.5.cloned.1.call-update) | async-done | bytes 524304 | tf_op jit(solution)/shard_map/reduce_scatter | solution.py:37
  207.1 0.0 reduce-scatter.3.cloned.1.call-start
  207.1 15.1 %fusion.9 = bf16[2,1024,1024]{1,2,0:T(8,128)(2,1)} fusion(bf16[2,4,1024,256]{3,2,1,0:T(8,128)(2,1)} %param.11, bf16[2,4,1024,256]{3,2,1,0:T(8,128)(2,1)} %param.12, bf16[4,1024,1024]{2,1,0:T(8,128)(2,1)} %all-gather.4.cloned.1.call-done, pred[2,4,256]{2,1,0:T(4,128)(4,1)S(1)} %iota_compare_fusion), kind=kOutput, calls=%fused_computation.8 | convolution fusion | flops 8596226048 | bytes 20973568 | tf_op jit(solution)/shard_map/ijbr,ijrn->ibn/dot_general | solution.py:24
  222.3 58.9 %all-reduce.2.cloned.1.call-done = bf16[1024,256]{0,1:T(8,128)(2,1)} async-done(((bf16[1024,256]{0,1:T(8,128)(2,1)}), bf16[1024,256]{0,1:T(8,128)(2,1)}) %all-reduce.2.cloned.1.call-update) | async-done | bytes 524304 | tf_op jit(solution)/shard_map/psum | solution.py:40
  281.2 1.5 fusion.24
  282.6 46.7 %reduce-scatter.3.cloned.1.call-done = bf16[2,1024,256]{1,2,0:T(8,128)(2,1)} async-done(((bf16[2,1024,1024]{1,2,0:T(8,128)(2,1)}), bf16[2,1024,256]{1,2,0:T(8,128)(2,1)}) %reduce-scatter.3.cloned.1.call-update) | async-done | bytes 1048592 | tf_op jit(solution)/shard_map/reduce_scatter | solution.py:44
  329.3 2.3 fusion.20
  331.6 1.3 copy.8
  (15 shorter events, 0.1 us)
Async XLA Ops:
  6.5 127.2 %all-gather.4.cloned.1.call-start = ((), (), s32[]{:S(2)}) async-start(), calls=%async_computation.2 | async-start | bytes 9437184 | tf_op jit(solution)/shard_map/all_gather | solution.py:14
  7.3 144.1 %all-gather.6.cloned.1.call-start = ((), (), s32[]{:S(2)}) async-start(), calls=%async_computation.4 | async-start | bytes 1310720 | tf_op jit(solution)/shard_map/all_gather | solution.py:16
  8.0 161.7 %all-gather.8.cloned.1.call-start = ((), (), s32[]{:S(2)}) async-start(), calls=%async_computation.5 | async-start | bytes 1310720 | tf_op jit(solution)/shard_map/all_gather | solution.py:17
  8.7 198.3 %reduce-scatter.5.cloned.1.call-start = ((), (), s32[]{:S(2)}) async-start(), calls=%async_computation.6 | async-start | bytes 2621440 | tf_op jit(solution)/shard_map/reduce_scatter | solution.py:37
  169.7 6.2 %copy-start.2 = (s32[2,4]{1,0:T(2,128)S(1)}, s32[2,4]{1,0:T(2,128)}, u32[]{:S(2)}) copy-start(s32[2,4]{1,0:T(2,128)} %param.13) | copy-start | bytes 100
  175.9 105.3 %all-reduce.2.cloned.1.call-start = ((), (), s32[]{:S(2)}) async-start(), calls=%async_computation.7 | async-start | bytes 1048576 | tf_op jit(solution)/shard_map/psum | solution.py:40
  207.1 122.2 %reduce-scatter.3.cloned.1.call-start = ((), (), s32[]{:S(2)}) async-start(), calls=%async_computation.3 | async-start | bytes 5242880 | tf_op jit(solution)/shard_map/reduce_scatter | solution.py:44
  222.2 58.9 %copy-start.1 = (bf16[2,1024,256]{2,1,0:T(8,128)(2,1)S(1)}, bf16[2,1024,256]{2,1,0:T(8,128)(2,1)}, u32[]{:S(2)}) copy-start(bf16[2,1024,256]{2,1,0:T(8,128)(2,1)} %all-gather.8.cloned.1.call-done) | copy-start | bytes 3145732
  222.2 107.1 %copy-start = (bf16[2,1024,256]{2,1,0:T(8,128)(2,1)S(1)}, bf16[2,1024,256]{2,1,0:T(8,128)(2,1)}, u32[]{:S(2)}) copy-start(bf16[2,1024,256]{2,1,0:T(8,128)(2,1)} %all-gather.6.cloned.1.call-done) | copy-start | bytes 3145732
Sparse Core Ops, SparseCore 0:
  9.5 124.1 all-gather.3
  135.3 16.0 all-gather.5
  153.0 16.7 all-gather.7
  176.0 31.0 reduce-scatter.4
  210.7 70.4 all-reduce.1
  283.5 45.7 reduce-scatter.2
where the time goes:
time: 343 us; the launch traced here: 340 us
  waiting for transfers between devices  286 us (83%)
  matrix products  25 us (7%)
  local copies, waits for them, and re-layouts  15.2 us (4%)
  between operations  13.5 us (4%)
    all_gather x1, waiting for transfers between devices, shards(): gathered = lax.all_gather(x_rhs, 'row', axis=1, tiled=True)  124 us
    psum x1, waiting for transfers between devices, shards(): sweep = lax.psum(sweep_share, 'row').astype(jnp.float32)  58.9 us
    reduce_scatter x1, waiting for transfers between devices, shards(): lax.psum_scatter(base_sum.astype(jnp.bfloat16), 'col', scatter_dimension=...  46.7 us
    reduce_scatter x1, waiting for transfers between devices, shards(): lax.psum_scatter(sweep_part.astype(jnp.bfloat16), 'col', scatter_dimensio...  31 us
    all_gather x1, waiting for transfers between devices, shards(): lax.all_gather(panel_v, 'col', axis=1, tiled=True)  18.3 us
    dot_general x1, matrix products, shards(): jnp.einsum('ijbr,ijrn->ibn', tile_p, tile_proj, preferred_element_type=jn...  15.1 us
    gather x3, local copies, waits for them, and re-layouts, shards(): picked = jnp.take(gathered, where_rhs, axis=0)  13.1 us
  transfers between devices with their start and end apart: 6, of which 6 were waited for; matrix products, arithmetic and copies ran while one was open for 9% of the time, Pallas kernels for 0%

commit v1 on v0

--- a/solution.py
+++ b/solution.py
@@ -1,10 +1,19 @@
+import functools
+
 import jax
 import jax.numpy as jnp
 from jax import lax
+from jax.experimental import pallas as pl
+from jax.experimental.pallas import tpu as pltpu
 from jax.sharding import PartitionSpec as P
 
-
-def shards(x_rhs, panel_u, panel_v, panel_rank, tile_p, tile_q, tile_rank):
+BF16 = jnp.bfloat16
+F32 = jnp.float32
+MESH = pl.DeviceIdType.MESH
+UP, DOWN, ACROSS = 0, 1, 2
+
+
+def plain(x_rhs, panel_u, panel_v, panel_rank, tile_p, tile_q, tile_rank):
     exact = lax.Precision.HIGHEST
     row_at = lax.axis_index("row")
     col_at = lax.axis_index("col")
@@ -47,9 +56,357 @@
     return (summed - late_term).astype(jnp.bfloat16)
 
 
+def dot(a, b):
+    return jnp.dot(a, b, preferred_element_type=F32)
+
+
+def kernel(
+    n_row, n_col,
+    tile_rank, panel_rank, x_in, u_in, v_in, p_in, q_in,
+    out,
+    xg, pv, qv, qt, ug, vg, ut, vt, acc, sweep_acc, sbuf, rbuf, swb, swr, swg,
+    x_send, x_recv, uv_send, uv_recv, b_send, b_recv, sw_send, sw_recv, g_send, g_recv, local,
+):
+    t_rows, t_cols, order, rank_cap = pv.shape
+    x_rows = xg.shape[3]
+    width = xg.shape[4]
+    u_rows = ug.shape[2]
+    steps = n_col
+    line = n_row // 2
+    row = lax.axis_index("row")
+    col = lax.axis_index("col")
+    z, x = row // 2, row % 2
+    inside = (row * t_rows) // t_cols == col
+    first = lax.rem(row * t_rows, t_cols)
+
+    def owner(s):
+        return lax.rem(col + 1 + s, n_col)
+
+    def x_local(s):
+        at = pl.multiple_of(owner(s) * width, width)
+        return pltpu.make_async_copy(x_in.at[:, :, pl.ds(at, width)], xg.at[s, row], local.at[s])
+
+    q_local = pltpu.make_async_copy(q_in, qv, local.at[steps])
+    p_local = pltpu.make_async_copy(p_in, pv, local.at[steps + 1])
+    u_local = pltpu.make_async_copy(u_in, ug.at[col], local.at[steps + 2])
+    v_local = pltpu.make_async_copy(v_in, vg.at[col], local.at[steps + 3])
+    x_local(0).start()
+    u_local.start()
+    v_local.start()
+    for s in range(1, steps):
+        x_local(s).start()
+    q_local.start()
+    p_local.start()
+
+    barrier = pltpu.get_barrier_semaphore()
+
+    @pl.loop(0, n_row * n_col)
+    def _(k):
+        @pl.when(k != row * n_col + col)
+        def _():
+            pl.semaphore_signal(
+                barrier, inc=1, device_id=(k // n_col, lax.rem(k, n_col)), device_id_type=MESH
+            )
+
+    pl.semaphore_wait(barrier, n_row * n_col - 1)
+
+    def x_copy(s, k, way):
+        target = {UP: row + 2, DOWN: row - 2, ACROSS: row + 1 - 2 * x}[way]
+        return pltpu.make_async_remote_copy(
+            src_ref=xg.at[s, k], dst_ref=xg.at[s, k],
+            send_sem=x_send.at[s, k, way], recv_sem=x_recv.at[s, k],
+            device_id=(target, col), device_id_type=MESH,
+        )
+
+    def own_sends(s):
+        x_local(s).wait()
+        x_copy(s, row, ACROSS).start()
+
+        @pl.when(z + 1 < line)
+        def _():
+            x_copy(s, row, UP).start()
+
+        @pl.when(z > 0)
+        def _():
+            x_copy(s, row, DOWN).start()
+
+    def forward(s, d):
+        @pl.when(z - d >= 0)
+        def _():
+            k = row - 2 * d
+            x_copy(s, k, ACROSS).wait_recv()
+            x_copy(s, k, ACROSS).start()
+
+            @pl.when(z + 1 < line)
+            def _():
+                x_copy(s, k, UP).start()
+
+        @pl.when(z + d < line)
+        def _():
+            k = row + 2 * d
+            x_copy(s, k, ACROSS).wait_recv()
+            x_copy(s, k, ACROSS).start()
+
+            @pl.when(z > 0)
+            def _():
+                x_copy(s, k, DOWN).start()
+
+    def uv_copy(which, d, slot):
+        ref = (ug, vg)[which]
+        return pltpu.make_async_remote_copy(
+            src_ref=ref.at[slot], dst_ref=ref.at[slot],
+            send_sem=uv_send.at[which, d], recv_sem=uv_recv.at[which, d],
+            device_id=(row, lax.rem(col + d, n_col)), device_id_type=MESH,
+        )
+
+    own_sends(0)
+    u_local.wait()
+    v_local.wait()
+    for d in range(1, n_col):
+        uv_copy(0, d, col).start()
+        uv_copy(1, d, col).start()
+    own_sends(1)
+
+    q_local.wait()
+
+    @pl.loop(0, t_rows * t_cols)
+    def _(k):
+        i, j = k // t_cols, lax.rem(k, t_cols)
+        keep = lax.broadcasted_iota(jnp.int32, (rank_cap, u_rows), 0) < tile_rank[i, j]
+        for b in range(order // u_rows):
+            at = pl.ds(b * u_rows, u_rows)
+            qt[i, j, :, at] = jnp.where(keep, qv[i, j, at, :].T, jnp.zeros((), BF16))
+
+    p_local.wait()
+    for d in range(1, n_col):
+        slot = lax.rem(col + n_col - d, n_col)
+        uv_copy(0, d, slot).wait_recv()
+        uv_copy(1, d, slot).wait_recv()
+
+    @pl.loop(0, t_rows)
+    def _(i):
+        keep = (
+            lax.broadcasted_iota(jnp.int32, (rank_cap, u_rows), 0) < panel_rank[row * t_rows + i]
+        )
+        for b in range(n_col):
+            at = pl.ds(b * u_rows, u_rows)
+            ut[i, :, at] = jnp.where(keep, ug[b, i].T, jnp.zeros((), BF16))
+            vt[i, :, at] = jnp.where(keep, vg[b, i].T, jnp.zeros((), BF16))
+
+    def b_copy(s):
+        return pltpu.make_async_remote_copy(
+            src_ref=sbuf.at[s], dst_ref=rbuf.at[s],
+            send_sem=b_send.at[s], recv_sem=b_recv.at[s],
+            device_id=(row, owner(s)), device_id_type=MESH,
+        )
+
+    def sw_copy(s, k):
+        return pltpu.make_async_remote_copy(
+            src_ref=swb.at[s, k], dst_ref=swr.at[row],
+            send_sem=sw_send.at[s, k], recv_sem=sw_recv.at[row],
+            device_id=(k, owner(s)), device_id_type=MESH,
+        )
+
+    def compute(s):
+        for k in range(line):
+            x_copy(s, 2 * k + 1 - x, ACROSS).wait_recv()
+
+        @pl.when(inside)
+        def _():
+            for i in range(t_rows):
+                block = xg[s, :, first + i].reshape(order, width)
+                proj = dot(ut[i], block).astype(BF16)
+                term = dot(vg[:, i].reshape(order, rank_cap), proj)
+                if i == 0:
+                    sweep_acc[...] = term
+                else:
+                    sweep_acc[...] += term
+            swb[s] = sweep_acc[...].astype(BF16).reshape(n_row, x_rows, width)
+
+            @pl.loop(0, n_row)
+            def _(k):
+                mine = jnp.logical_and(k == row, s == steps - 1)
+
+                @pl.when(mine)
+                def _():
+                    swr[row] = swb[s, row]
+
+                @pl.when(jnp.logical_not(mine))
+                def _():
+                    sw_copy(s, k).start()
+
+        @pl.loop(0, t_rows)
+        def _(i):
+            total = None
+            for j in range(t_cols):
+                proj = dot(qt[i, j], xg[s, :, j].reshape(order, width)).astype(BF16)
+                term = dot(pv[i, j], proj)
+                total = term if total is None else total + term
+
+            acc[i] = total
+
+            @pl.when(s < steps - 1)
+            def _():
+                sbuf[s, i] = acc[i].astype(BF16)
+
+        @pl.when(s < steps - 1)
+        def _():
+            b_copy(s).start()
+
+    @pl.loop(0, steps + 1)
+    def _(s):
+        @pl.when(s < steps)
+        def _():
+            forward(s, 1)
+
+        @pl.when(s + 2 < steps)
+        def _():
+            own_sends(s + 2)
+
+        @pl.when(s > 0)
+        def _():
+            compute(s - 1)
+
+        @pl.when(s < steps)
+        def _():
+            for d in range(2, line):
+                forward(s, d)
+
+    for k in range(n_row):
+        @pl.when(jnp.logical_not(jnp.logical_and(inside, k == row)))
+        def _():
+            pltpu.make_async_remote_copy(
+                src_ref=swr.at[k], dst_ref=swr.at[k],
+                send_sem=sw_send.at[0, 0], recv_sem=sw_recv.at[k],
+                device_id=(row, col), device_id_type=MESH,
+            ).wait_recv()
+
+    swg[row] = functools.reduce(lambda a, k: a + swr[k].astype(F32), range(1, n_row), swr[0].astype(F32)).astype(BF16)
+
+    def g_copy(d, slot):
+        return pltpu.make_async_remote_copy(
+            src_ref=swg.at[slot], dst_ref=swg.at[slot],
+            send_sem=g_send.at[d], recv_sem=g_recv.at[d],
+            device_id=(lax.rem(row + d, n_row), col), device_id_type=MESH,
+        )
+
+    for d in range(1, n_row):
+        g_copy(d, row).start()
+    for s in range(steps - 1):
+        b_copy(s).wait_recv()
+
+    @pl.loop(0, t_rows)
+    def _(i):
+        total = acc[i]
+        for s in range(steps - 1):
+            total = total + rbuf[s, i].astype(F32)
+        acc[i] = total
+
+    for d in range(1, n_row):
+        g_copy(d, lax.rem(row + n_row - d, n_row)).wait_recv()
+
+    @pl.loop(0, t_rows)
+    def _(i):
+        back = dot(vt[i], swg[...].reshape(order, width)).astype(BF16)
+        late = dot(ug[:, i].reshape(order, rank_cap), back)
+        out[i] = (acc[i] - late).astype(BF16)
+
+    @pl.loop(0, steps)
+    def _(s):
+        for m in range(line):
+            k = 2 * m + x
+            x_copy(s, k, ACROSS).wait_send()
+
+            @pl.when(jnp.logical_and(m <= z, z + 1 < line))
+            def _():
+                x_copy(s, k, UP).wait_send()
+
+            @pl.when(jnp.logical_and(m >= z, z > 0))
+            def _():
+                x_copy(s, k, DOWN).wait_send()
+
+        @pl.when(s < steps - 1)
+        def _():
+            b_copy(s).wait_send()
+
+        @pl.when(inside)
+        def _():
+            @pl.loop(0, n_row)
+            def _(k):
+                @pl.when(jnp.logical_not(jnp.logical_and(k == row, s == steps - 1)))
+                def _():
+                    sw_copy(s, k).wait_send()
+
+    for d in range(1, n_col):
+        uv_copy(0, d, col).wait_send()
+        uv_copy(1, d, col).wait_send()
+    for d in range(1, n_row):
+        g_copy(d, row).wait_send()
+
+
+def shards(n_row, n_col, x_rhs, panel_u, panel_v, panel_rank, tile_p, tile_q, tile_rank):
+    t_rows, t_cols, order, rank_cap = tile_p.shape
+    x_rows, n_rhs = x_rhs.shape[1:]
+    u_rows = panel_u.shape[1]
+    width = n_rhs // n_col
+    fits = (
+        width % 128 == 0
+        and x_rows % 16 == 0
+        and u_rows % 128 == 0
+        and n_row % 2 == 0
+        and n_row > 2
+        and n_col > 1
+        and t_cols % t_rows == 0
+        and n_rhs % n_col == 0
+    )
+    if not fits:
+        return plain(x_rhs, panel_u, panel_v, panel_rank, tile_p, tile_q, tile_rank)
+    dma = pltpu.SemaphoreType.DMA
+    flops = 4 * order * rank_cap * n_rhs * t_rows * (t_cols + 1)
+    return pl.pallas_call(
+        functools.partial(kernel, n_row, n_col),
+        out_shape=jax.ShapeDtypeStruct((t_rows, order, width), BF16),
+        in_specs=[pl.BlockSpec(memory_space=pltpu.SMEM)] * 2
+        + [pl.BlockSpec(memory_space=pl.ANY)] * 5,
+        out_specs=pl.BlockSpec(memory_space=pltpu.VMEM),
+        scratch_shapes=[
+            pltpu.VMEM((n_col, n_row, t_cols, x_rows, width), BF16),
+            pltpu.VMEM(tile_p.shape, BF16),
+            pltpu.VMEM(tile_q.shape, BF16),
+            pltpu.VMEM((t_rows, t_cols, rank_cap, order), BF16),
+            pltpu.VMEM((n_col, t_rows, u_rows, rank_cap), BF16),
+            pltpu.VMEM((n_col, t_rows, u_rows, rank_cap), BF16),
+            pltpu.VMEM((t_rows, rank_cap, order), BF16),
+            pltpu.VMEM((t_rows, rank_cap, order), BF16),
+            pltpu.VMEM((t_rows, order, width), F32),
+            pltpu.VMEM((order, width), F32),
+            pltpu.VMEM((n_col - 1, t_rows, order, width), BF16),
+            pltpu.VMEM((n_col - 1, t_rows, order, width), BF16),
+            pltpu.VMEM((n_col, n_row, x_rows, width), BF16),
+            pltpu.VMEM((n_row, x_rows, width), BF16),
+            pltpu.VMEM((n_row, x_rows, width), BF16),
+            dma((n_col, n_row, 3)),
+            dma((n_col, n_row)),
+            dma((2, n_col)),
+            dma((2, n_col)),
+            dma((n_col,)),
+            dma((n_col,)),
+            dma((n_col, n_row)),
+            dma((n_row,)),
+            dma((n_row,)),
+            dma((n_row,)),
+            dma((n_col + 4,)),
+        ],
+        compiler_params=pltpu.CompilerParams(
+            collective_id=0, has_side_effects=True, vmem_limit_bytes=56 * 2**20
+        ),
+        cost_estimate=pl.CostEstimate(flops=flops, bytes_accessed=20 * 2**20, transcendentals=0),
+    )(tile_rank, panel_rank, x_rhs, panel_u, panel_v, tile_p, tile_q)
+
+
 def solution(mesh):
     return jax.shard_map(
-        shards,
+        functools.partial(shards, mesh.shape["row"], mesh.shape["col"]),
         mesh=mesh,
         in_specs=(
             P("col", "row", None),

time: 343 us -> 130 us (0.38)
  waiting for transfers between devices: 286 us -> 0 us
  Pallas kernels: 0 us -> 128 us
  matrix products: 25 us -> 0 us
  between operations: 13.5 us -> 0.01 us
  local copies, waits for them, and re-layouts: 15.2 us -> 2.26 us
    all_gather x3 -> x0, waiting for transfers between devices: 147 us -> none  [the longest x1 124 us: shards(): gathered = lax.all_gather(x_rhs, 'row', axis=1, tiled=True)]
    pallas_call x0 -> x1, Pallas kernels: none -> 128 us  [shards(): pl.pallas_call(functools.partial(kernel, n_row, n_col), out_shape=jax.Sha...]
    reduce_scatter x2 -> x0, waiting for transfers between devices: 77.7 us -> none  [the longest x1 46.7 us: shards(): lax.psum_scatter(base_sum.astype(jnp.bfloat16), 'col', scatter_dimension=...]
    psum x1 -> x0, waiting for transfers between devices: 58.9 us -> none  [shards(): sweep = lax.psum(sweep_share, 'row').astype(jnp.float32)]
    dot_general x4 -> x0, matrix products: 25 us -> none  [the longest x1 15.1 us: shards(): jnp.einsum('ijbr,ijrn->ibn', tile_p, tile_proj, preferred_element_type=jn...]
    gather x3 -> x0, local copies, waits for them, and re-layouts: 13.1 us -> none  [shards(): picked = jnp.take(gathered, where_rhs, axis=0)]
  transfers between devices with their start and end apart: 6 -> 0, of which waited for: 6 -> 0; matrix products, arithmetic and copies ran while one was open for 9% -> 0% of each run, Pallas kernels for 0% -> 0%
where the time goes in v1:
time: 130 us
  Pallas kernels  128 us (98%)
  local copies, waits for them, and re-layouts  2.26 us (2%)
    pallas_call x1, Pallas kernels, shards(): pl.pallas_call(functools.partial(kernel, n_row, n_col), out_shape=jax.Sha...  128 us

profile of v1, /device:TPU:29, one launch (start us, length us, event | category | flops | bytes accessed | tf_op | source)
XLA Modules:
  0.0 130.1 jit_solution(13920647768059911194)
XLA Ops:
  0.0 127.8 %shard_map.73 = bf16[2,1024,256]{2,1,0:T(8,128)(2,1)} custom-call(s32[2,4]{1,0:T(2,128)} %tile_rank.1, s32[16]{0:T(128)} %panel_rank.1, bf16[4,128,1024]{2,1,0:T(8,128)(2,1)} %x_in.1, bf16[2,256,256]{2,1,0:T(8,128)(2,1)} %u_in.1, bf16[2,256,256]{2,1,0:T(8,128)(2,1)} %v_in.1, bf16[2,4,1024,256]{3,2,1,0:T(8,128)(2,1)} %p_in.1, bf16[2,4,1024,256]{3,2,1,0:T(8,128)(2,1)} %q_in.1), custom_call_target="tpu_custom_call" | custom-call | flops 10737418240 | bytes 20971520 | tf_op jit(solution)/shard_map/pallas_call | solution.py:366
  127.8 2.3 %copy.9 = bf16[2,1024,256]{2,1,0:T(8,128)(2,1)} copy(bf16[2,1024,256]{2,1,0:T(8,128)(2,1)} %shard_map.73) | data formatting | bytes 2097152
